TPU v7x, 32 devices: a whole 2x2x4 slice. The times are simulated.
32 devices in a mesh: expert: 8 (over z, x), panel: 4 (over y, core).
Axes of the slice: x: 2, y: 2, z: 4, core: 2. Of those that a mesh axis runs over, the one named last changes fastest.
Arguments:
- lower_factor: bfloat16 [28672, 3584], P(('expert', 'panel')), parts along dimension 0, may hold values from -1 to 2.5, as said below
- inverses: float32 [128, 224, 224], P(('expert', 'panel')), parts along dimension 0, may hold values from -1 to 1.3, as said below
- probes: bfloat16 [28672, 512], P(('expert', 'panel')), parts along dimension 0, may hold values from -6 to 6
Outputs:
- whitened: float32 [28672, 512], P(('expert', 'panel')), parts along dimension 0
There are 8 independent parts, one for each index of `expert`. A program takes and returns all parts, laid end to end along the dimension named above; each array names one. Nothing has to cross between parts.
Inputs may be any that keep to these rules, and one draw needn't show every extreme that they name: lower_factor is lower triangular with a positive diagonal. inverses[b] is lower triangular, the inverse of the b-th diagonal 224 x 224 block of lower_factor up to float32 rounding.
All inputs are finite; a program needn't handle non-finite values.
Results may differ from a plain program's by a relative error of at most 0.0011.
Values may be sent and summed in bfloat16 or wider, within the bound.
A program may use at most 64 MiB of HBM per device.

v0:
```python
import jax
import jax.numpy as jnp
from jax import lax
from jax.sharding import PartitionSpec as P


def broadcast(x, axis, root):
    mine = lax.axis_index(axis) == root
    return lax.psum(jnp.where(mine, x, jnp.zeros_like(x)), axis)


def solve_panel(pending, lower_factor, inverses, position):
    block_size = inverses.shape[1]
    block_count = inverses.shape[0]
    panel_rows = lower_factor.shape[0]
    pieces = []
    halves = []
    for block_index in range(block_count):
        first = block_index * block_size
        residual = pending[first : first + block_size]
        if block_index > 0:
            coupling = lax.dynamic_slice_in_dim(
                lower_factor[first : first + block_size], position * panel_rows, first, 1
            )
            residual = residual - jnp.dot(
                coupling, jnp.concatenate(halves, 0), preferred_element_type=jnp.float32
            )
        solved = jnp.dot(
            inverses[block_index],
            residual,
            precision=lax.Precision.HIGHEST,
            preferred_element_type=jnp.float32,
        )
        pieces.append(solved)
        halves.append(solved.astype(jnp.bfloat16))
    return jnp.concatenate(pieces, 0)


def per_device(lower_factor, inverses, probes):
    panel_rows = probes.shape[0]
    position = lax.axis_index("panel")
    panels = lax.axis_size("panel")
    initial = probes.astype(jnp.float32)

    def own_solve(current, before):
        return solve_panel(current, lower_factor, inverses, position)

    def keep_old(current, before):
        return before

    def advance(moment, loop_state):
        pending, solved = loop_state
        solved = lax.cond(position == moment, own_solve, keep_old, pending, solved)
        shared = broadcast(solved.astype(jnp.bfloat16), "panel", moment)
        coupling = lax.dynamic_slice_in_dim(lower_factor, moment * panel_rows, panel_rows, 1)
        change = jnp.dot(coupling, shared, preferred_element_type=jnp.float32)
        pending = jnp.where(position > moment, pending - change, pending)
        return (pending, solved)

    pending, solved = lax.fori_loop(0, panels, advance, (initial, jnp.zeros_like(initial)))
    return solved


def solution(mesh):
    return jax.shard_map(
        per_device,
        mesh=mesh,
        in_specs=(
            P(("expert", "panel"), None),
            P(("expert", "panel"), None, None),
            P(("expert", "panel"), None),
        ),
        out_specs=P(("expert", "panel"), None),
        check_vma=False,
    )
```

profile of v0, /device:TPU:29, one launch (start us, length us, event | category | flops | bytes accessed | tf_op | source)
XLA Modules:
  0.0 207.6 jit_solution(12440532234549356690)
XLA Ops:
  6.5 0.0 copy-start
  6.5 1.5 convert_element_type.32
  8.1 1.5 broadcast_in_dim.3
  9.5 0.0 copy-done
  9.5 191.5 %while.18 = (s32[]{:T(128)}, f32[896,512]{1,0:T(8,128)S(1)}, f32[896,512]{1,0:T(8,128)}, s32[]{:T(128)}, bf16[896,3584]{1,0:T(8,128)(2,1)}, /*index=5*/f32[4,224...) while((s32[]{:T(128)}, f32[896,512]{1,0:T(8,128)S(1)}, ...), condition=%wide.region_4.5_spmd, body=%wide.region_0.4_spmd.sunk | while | flops 2370830336 | bytes 37847384 | solution.py:60
  9.5 0.0 all-reduce.2.cloned.1.call-start
  9.5 2.5 %convert_select_fusion.2 = bf16[896,512]{1,0:T(8,128)(2,1)} fusion(f32[896,512]{1,0:T(8,128)} %get-tuple-element.232, pred[]{:T(512)S(6)} %eq.17), kind=kLoop, calls=%fused_computation.36.clone.1 | loop fusion | flops 917504 | bytes 2752513 | tf_op jit(solution)/shard_map/while/body/eval_jaxpr/jit(_where)/select_n | solution.py:9
  12.1 0.0 all-reduce.2.cloned.1.call-update
  12.1 41.9 %all-reduce.2.cloned.1.call-done = bf16[896,512]{1,0:T(8,128)(2,1)} async-done(((bf16[896,512]{1,0:T(8,128)(2,1)}), bf16[896,512]{1,0:T(8,128)(2,1)}) %all-reduce.2.cloned.1.call-update) | async-done | bytes 917520 | tf_op jit(solution)/shard_map/while/body/eval_jaxpr/psum | solution.py:9
  54.0 3.0 %subtract_select_fusion.2 = f32[896,512]{1,0:T(8,128)S(1)} fusion(f32[896,512]{1,0:T(8,128)S(1)} %get-tuple-element.211, bf16[896,512]{1,0:T(8,128)(2,1)} %all-reduce.2.cloned.1.call-done, bf16[896,3584]{1,0:T(8,128)(2,1)} %get-tuple-element.225, s32[]{:T(128)S(6)} %select_n.57, pred[]{:T(512)S(6)} %gt.8), kind=kOutput, calls=%fused_computation.33.clone.1 | convolution fusion | flops 823001088 | bytes 6193157 | tf_op jit(solution)/shard_map/while/body/eval_jaxpr/dot_general | solution.py:56
  56.9 0.0 all-reduce.2.cloned.1.call-start
  57.0 2.5 %convert_select_fusion.2 = bf16[896,512]{1,0:T(8,128)(2,1)} fusion(f32[896,512]{1,0:T(8,128)} %get-tuple-element.232, pred[]{:T(512)S(6)} %eq.17), kind=kLoop, calls=%fused_computation.36.clone.1 | loop fusion | flops 917504 | bytes 2752513 | tf_op jit(solution)/shard_map/while/body/eval_jaxpr/jit(_where)/select_n | solution.py:9
  59.6 0.0 all-reduce.2.cloned.1.call-update
  59.6 41.8 %all-reduce.2.cloned.1.call-done = bf16[896,512]{1,0:T(8,128)(2,1)} async-done(((bf16[896,512]{1,0:T(8,128)(2,1)}), bf16[896,512]{1,0:T(8,128)(2,1)}) %all-reduce.2.cloned.1.call-update) | async-done | bytes 917520 | tf_op jit(solution)/shard_map/while/body/eval_jaxpr/psum | solution.py:9
  101.4 3.0 %subtract_select_fusion.2 = f32[896,512]{1,0:T(8,128)S(1)} fusion(f32[896,512]{1,0:T(8,128)S(1)} %get-tuple-element.211, bf16[896,512]{1,0:T(8,128)(2,1)} %all-reduce.2.cloned.1.call-done, bf16[896,3584]{1,0:T(8,128)(2,1)} %get-tuple-element.225, s32[]{:T(128)S(6)} %select_n.57, pred[]{:T(512)S(6)} %gt.8), kind=kOutput, calls=%fused_computation.33.clone.1 | convolution fusion | flops 823001088 | bytes 6193157 | tf_op jit(solution)/shard_map/while/body/eval_jaxpr/dot_general | solution.py:56
  104.4 0.0 all-reduce.2.cloned.1.call-start
  104.4 2.5 %convert_select_fusion.2 = bf16[896,512]{1,0:T(8,128)(2,1)} fusion(f32[896,512]{1,0:T(8,128)} %get-tuple-element.232, pred[]{:T(512)S(6)} %eq.17), kind=kLoop, calls=%fused_computation.36.clone.1 | loop fusion | flops 917504 | bytes 2752513 | tf_op jit(solution)/shard_map/while/body/eval_jaxpr/jit(_where)/select_n | solution.py:9
  107.0 0.0 all-reduce.2.cloned.1.call-update
  107.0 43.1 %all-reduce.2.cloned.1.call-done = bf16[896,512]{1,0:T(8,128)(2,1)} async-done(((bf16[896,512]{1,0:T(8,128)(2,1)}), bf16[896,512]{1,0:T(8,128)(2,1)}) %all-reduce.2.cloned.1.call-update) | async-done | bytes 917520 | tf_op jit(solution)/shard_map/while/body/eval_jaxpr/psum | solution.py:9
  150.1 3.0 %subtract_select_fusion.2 = f32[896,512]{1,0:T(8,128)S(1)} fusion(f32[896,512]{1,0:T(8,128)S(1)} %get-tuple-element.211, bf16[896,512]{1,0:T(8,128)(2,1)} %all-reduce.2.cloned.1.call-done, bf16[896,3584]{1,0:T(8,128)(2,1)} %get-tuple-element.225, s32[]{:T(128)S(6)} %select_n.57, pred[]{:T(512)S(6)} %gt.8), kind=kOutput, calls=%fused_computation.33.clone.1 | convolution fusion | flops 823001088 | bytes 6193157 | tf_op jit(solution)/shard_map/while/body/eval_jaxpr/dot_general | solution.py:56
  153.1 0.0 all-reduce.2.cloned.1.call-start
  153.2 7.5 %conditional.2 = (f32[896,512]{1,0:T(8,128)}) conditional(s32[]{:T(128)} %convert_element_type.40, f32[896,512]{1,0:T(8,128)} %get-tuple-element.212, (f32[4,224,224]{2,1,0:T(8,128)S(1)}, f32[896,512]{1,0:T(8,128)S(1)}, bf16[896,3584]{1,0:T(8,128)(2,1)}, s32[]{:T(128)}) %tuple.54), branch_computations={%region_1.0_spmd, %region_2.0_spmd} | conditional | flops 1546452992 | bytes 23396418 | solution.py:53
  153.2 0.6 fusion.32
  153.7 2.7 %fusion.31 = (bf16[224,3584]{1,0:T(8,128)(2,1)S(1)}, bf16[224,3584]{1,0:T(8,128)(2,1)S(1)}, bf16[224,3584]{1,0:T(8,128)(2,1)S(1)}) fusion(bf16[896,3584]{1,0:T(8,128)(2,1)} %get-tuple-element.130), kind=kLoop, calls=%fused_computation.38 | loop fusion | bytes 9633792 | tf_op jit(solution)/shard_map/while/body/eval_jaxpr/cond/branch_1_fun/slice | solution.py:23
  156.4 0.3 convolution_subtract_fusion.1
  156.7 0.6 fusion.33
  157.3 0.3 convolution_subtract_fusion.2
  157.7 0.6 fusion.34
  158.2 0.4 convolution_subtract_fusion
  158.7 0.6 convolution_bitcast_fusion
  159.2 1.4 pad_maximum_fusion
  160.7 2.5 %convert_select_fusion.2 = bf16[896,512]{1,0:T(8,128)(2,1)} fusion(f32[896,512]{1,0:T(8,128)} %get-tuple-element.232, pred[]{:T(512)S(6)} %eq.17), kind=kLoop, calls=%fused_computation.36.clone.1 | loop fusion | flops 917504 | bytes 2752513 | tf_op jit(solution)/shard_map/while/body/eval_jaxpr/jit(_where)/select_n | solution.py:9
  163.2 0.0 all-reduce.2.cloned.1.call-update
  163.2 34.8 %all-reduce.2.cloned.1.call-done = bf16[896,512]{1,0:T(8,128)(2,1)} async-done(((bf16[896,512]{1,0:T(8,128)(2,1)}), bf16[896,512]{1,0:T(8,128)(2,1)}) %all-reduce.2.cloned.1.call-update) | async-done | bytes 917520 | tf_op jit(solution)/shard_map/while/body/eval_jaxpr/psum | solution.py:9
  198.1 3.0 %subtract_select_fusion.2 = f32[896,512]{1,0:T(8,128)S(1)} fusion(f32[896,512]{1,0:T(8,128)S(1)} %get-tuple-element.211, bf16[896,512]{1,0:T(8,128)(2,1)} %all-reduce.2.cloned.1.call-done, bf16[896,3584]{1,0:T(8,128)(2,1)} %get-tuple-element.225, s32[]{:T(128)S(6)} %select_n.57, pred[]{:T(512)S(6)} %gt.8), kind=kOutput, calls=%fused_computation.33.clone.1 | convolution fusion | flops 823001088 | bytes 6193157 | tf_op jit(solution)/shard_map/while/body/eval_jaxpr/dot_general | solution.py:56
  (3 shorter events, 0.0 us)
Async XLA Ops:
  6.5 3.0 %copy-start = (f32[4,224,224]{2,1,0:T(8,128)S(1)}, f32[4,224,224]{2,1,0:T(8,128)}, u32[]{:S(2)}) copy-start(f32[4,224,224]{2,1,0:T(8,128)} %param.8) | copy-start | bytes 2408452
  9.5 44.4 %all-reduce.2.cloned.1.call-start = ((), (), s32[]{:S(2)}) async-start(), calls=%async_computation | async-start | bytes 1835008 | tf_op jit(solution)/shard_map/while/body/eval_jaxpr/psum | solution.py:9
  56.9 44.4 %all-reduce.2.cloned.1.call-start = ((), (), s32[]{:S(2)}) async-start(), calls=%async_computation | async-start | bytes 1835008 | tf_op jit(solution)/shard_map/while/body/eval_jaxpr/psum | solution.py:9
  104.4 45.8 %all-reduce.2.cloned.1.call-start = ((), (), s32[]{:S(2)}) async-start(), calls=%async_computation | async-start | bytes 1835008 | tf_op jit(solution)/shard_map/while/body/eval_jaxpr/psum | solution.py:9
  153.1 45.0 %all-reduce.2.cloned.1.call-start = ((), (), s32[]{:S(2)}) async-start(), calls=%async_computation | async-start | bytes 1835008 | tf_op jit(solution)/shard_map/while/body/eval_jaxpr/psum | solution.py:9
Sparse Core Ops, SparseCore 0:
  12.7 41.1 all-reduce.1
  60.2 41.1 all-reduce.1
  107.6 42.4 all-reduce.1
  163.3 34.6 all-reduce.1
where the time goes:
time: 211 us; the launch traced here: 208 us
  waiting for transfers between devices  162 us (77%)
  matrix products  15.2 us (7%)
  other arithmetic  13.1 us (6%)
  between operations  13.1 us (6%)
  local copies, waits for them, and re-layouts  4.16 us (2%)
    psum x4, waiting for transfers between devices, broadcast(): return lax.psum(jnp.where(mine, x, jnp.zeros_like(x)), axis)  162 us
    dot_general x4, matrix products, advance(): change = jnp.dot(coupling, shared, preferred_element_type=jnp.float32)  11.9 us
    select_n x4, other arithmetic, broadcast(): return lax.psum(jnp.where(mine, x, jnp.zeros_like(x)), axis)  10.2 us
  transfers between devices with their start and end apart: 4, of which 4 were waited for; matrix products, arithmetic and copies ran while one was open for 0% of the time, Pallas kernels for 0%

commit v1 on v0

v1 whole, which is shorter than its diff:
```python
import functools

import jax
import jax.numpy as jnp
from jax import lax
from jax.experimental import pallas as pl
from jax.experimental.pallas import tpu as pltpu
from jax.sharding import PartitionSpec as P

MESH = pl.DeviceIdType.MESH
WIDTH = 256


def dot(a, b):
    return jnp.dot(a, b, preferred_element_type=jnp.float32)


def split(x):
    high = x.astype(jnp.bfloat16)
    return high, (x - high.astype(jnp.float32)).astype(jnp.bfloat16)


def kernel(
    panels, width, flat, lower, inverses, probes, out,
    factor, inverse, inv_high, inv_low, probe, result, solved, pending,
    load_sem, factor_sem, send_sem, recv_sem, out_sem,
):
    count, size = inverses.shape[0], inverses.shape[1]
    rows = count * size
    chunks = probes.shape[1] // width
    me = lax.axis_index("panel")
    after = lax.rem(me + 1, panels)
    has_next = me < panels - 1

    barrier = pltpu.get_barrier_semaphore()

    @pl.when(me > 0)
    def _():
        pl.semaphore_signal(barrier, inc=1, device_id={"panel": me - 1}, device_id_type=MESH)

    def load_factor(q):
        if flat:
            source = lower.at[:, pl.ds(pl.multiple_of(q * rows, 128), rows)]
        else:
            source = lower.at[q]
        return pltpu.make_async_copy(source, factor.at[q], factor_sem.at[q])

    load_inverse = pltpu.make_async_copy(inverses, inverse, load_sem.at[0])
    load_probe = pltpu.make_async_copy(probes, probe, load_sem.at[1])
    load_inverse.start()
    load_probe.start()
    load_factor(me).start()

    def start_factor(q, carry):
        load_factor(q).start()
        return carry

    lax.fori_loop(0, me, start_factor, 0)

    for c in range(chunks):
        solved[c, pl.ds(pl.multiple_of(me * rows, 16), rows)] = jnp.zeros((rows, width), jnp.bfloat16)
    load_inverse.wait()
    for b in range(count):
        inv_high[b], inv_low[b] = split(inverse[b])
    load_probe.wait()
    load_factor(me).wait()

    @pl.when(has_next)
    def _():
        pl.semaphore_wait(barrier, 1)

    def block_copy(c, g):
        block = solved.at[c, pl.ds(pl.multiple_of(g * size, 16), size)]
        return pltpu.make_async_remote_copy(
            src_ref=block,
            dst_ref=block,
            send_sem=send_sem.at[c, g],
            recv_sem=recv_sem.at[c, g],
            device_id={"panel": after},
            device_id_type=MESH,
        )

    def send(c, g):
        @pl.when(has_next)
        def _():
            block_copy(c, g).start()

    def out_copy(c):
        columns = pl.ds(pl.multiple_of(c * width, 128), width)
        return pltpu.make_async_copy(result.at[:, columns], out.at[:, columns], out_sem.at[c])

    def chunk(c, carry):
        columns = pl.ds(pl.multiple_of(c * width, 128), width)
        pending[...] = probe[:, columns].astype(jnp.float32)

        def earlier(q, carry):
            @pl.when(c == 0)
            def _():
                load_factor(q).wait()

            for j in range(count):
                block_copy(c, q * count + j).wait_recv()
                send(c, q * count + j)
            there = pl.ds(pl.multiple_of(q * rows, 16), rows)
            pending[...] -= dot(factor[q], solved[c, there])
            return carry

        lax.fori_loop(0, me, earlier, 0)

        for b in range(count):
            here = slice(b * size, (b + 1) * size)
            residual = pending[here]
            if b > 0:
                depth = min(rows, -(-b * size // 256) * 256)
                own = pl.ds(pl.multiple_of(me * rows, 16), depth)
                residual = residual - dot(factor[me, here, :depth], solved[c, own])
            high, low = split(residual)
            block = dot(inv_high[b], high) + (dot(inv_high[b], low) + dot(inv_low[b], high))
            result[here, columns] = block
            g = me * count + b
            solved[c, pl.ds(pl.multiple_of(g * size, 16), size)] = block.astype(jnp.bfloat16)
            send(c, g)
        out_copy(c).start()
        return carry

    lax.fori_loop(0, chunks, chunk, 0)

    def finish(c, carry):
        out_copy(c).wait()

        @pl.when(has_next)
        def _():
            def sent(g, carry):
                block_copy(c, g).wait_send()
                return carry

            lax.fori_loop(0, (me + 1) * count, sent, 0)

        return carry

    lax.fori_loop(0, chunks, finish, 0)


def per_device(lower_factor, inverses, probes):
    panels = lax.axis_size("panel")
    count, size, _ = inverses.shape
    rows, columns = probes.shape
    width = WIDTH if columns % WIDTH == 0 else columns
    chunks = columns // width
    flat = rows % 128 == 0
    if not flat:
        lower_factor = lower_factor.reshape(rows, panels, rows).transpose(1, 0, 2)
    bf16, f32 = jnp.bfloat16, jnp.float32
    dma = pltpu.SemaphoreType.DMA
    return pl.pallas_call(
        functools.partial(kernel, panels, width, flat),
        out_shape=jax.ShapeDtypeStruct((rows, columns), f32),
        in_specs=[pl.BlockSpec(memory_space=pl.ANY)] * 3,
        out_specs=pl.BlockSpec(memory_space=pl.ANY),
        scratch_shapes=[
            pltpu.VMEM((panels, rows, rows), bf16),
            pltpu.VMEM((count, size, size), f32),
            pltpu.VMEM((count, size, size), bf16),
            pltpu.VMEM((count, size, size), bf16),
            pltpu.VMEM((rows, columns), bf16),
            pltpu.VMEM((rows, columns), f32),
            pltpu.VMEM((chunks, panels * rows, width), bf16),
            pltpu.VMEM((rows, width), f32),
            dma((2,)),
            dma((panels,)),
            dma((chunks, panels * count)),
            dma((chunks, panels * count)),
            dma((chunks,)),
        ],
        compiler_params=pltpu.CompilerParams(
            collective_id=0, has_side_effects=True, vmem_limit_bytes=48 * 1024 * 1024
        ),
    )(lower_factor, inverses, probes)


def solution(mesh):
    return jax.shard_map(
        per_device,
        mesh=mesh,
        in_specs=(
            P(("expert", "panel"), None),
            P(("expert", "panel"), None, None),
            P(("expert", "panel"), None),
        ),
        out_specs=P(("expert", "panel"), None),
        check_vma=False,
    )
```

time: 211 us -> 36 us (0.17); the launches traced: 208 us -> 35.8 us
  waiting for transfers between devices: 162 us -> 0 us
  Pallas kernels: 0 us -> 32.2 us
  matrix products: 15.2 us -> 0 us
  other arithmetic: 13.1 us -> 0 us
  between operations: 13.1 us -> 0.01 us
    psum x4 -> x0, waiting for transfers between devices: 162 us -> none  [broadcast(): return lax.psum(jnp.where(mine, x, jnp.zeros_like(x)), axis)]
    pallas_call x0 -> x1, Pallas kernels: none -> 32.2 us  [per_device(): pl.pallas_call(functools.partial(kernel, panels, width, flat), out_shape=...]
    dot_general x11 -> x0, matrix products: 15.2 us -> none  [the longest x4 11.9 us: advance(): change = jnp.dot(coupling, shared, preferred_element_type=jnp.float32)]
    select_n x4 -> x0, other arithmetic: 10.2 us -> none  [broadcast(): return lax.psum(jnp.where(mine, x, jnp.zeros_like(x)), axis)]
    unnamed x2 -> x5, local copies, waits for them, and re-layouts: 0.01 us -> 3.59 us
    slice x1 -> x0, local copies, waits for them, and re-layouts: 2.7 us -> none  [solve_panel(): lower_factor[first:first + block_size]]
  transfers between devices with their start and end apart: 4 -> 0, of which waited for: 4 -> 0; matrix products, arithmetic and copies ran while one was open for 0% -> 0% of each run, Pallas kernels for 0% -> 0%
where the time goes in v1:
time: 36 us; the launch traced here: 35.8 us
  Pallas kernels  32.2 us (89%)
  local copies, waits for them, and re-layouts  3.59 us (10%)
    pallas_call x1, Pallas kernels, per_device(): pl.pallas_call(functools.partial(kernel, panels, width, flat), out_shape=...  32.2 us
    unnamed x5, local copies, waits for them, and re-layouts  3.59 us

profile of v1, /device:TPU:29, one launch (start us, length us, event | category | flops | bytes accessed | tf_op | source)
XLA Modules:
  0.0 35.8 jit_solution(7946750726767132576)
XLA Ops:
  0.0 0.0 copy-start
  0.0 1.2 %copy-done = f32[4,224,224]{2,1,0:T(8,128)S(1)} copy-done((f32[4,224,224]{2,1,0:T(8,128)S(1)}, f32[4,224,224]{2,1,0:T(8,128)}, u32[]{:S(2)}) %copy-start) | copy-done | bytes 802840
  1.2 0.0 copy-start.1
  1.2 1.2 %copy-done.1 = bf16[896,512]{1,0:T(8,128)(2,1)S(1)} copy-done((bf16[896,512]{1,0:T(8,128)(2,1)S(1)}, bf16[896,512]{1,0:T(8,128)(2,1)}, u32[]{:S(2)}) %copy-start.1) | copy-done | bytes 917528
  2.4 32.2 %shard_map.37 = f32[896,512]{1,0:T(8,128)S(1)} custom-call(bf16[896,3584]{1,0:T(8,128)(2,1)} %lower.1, f32[4,224,224]{2,1,0:T(8,128)S(1)} %copy-done, bf16[896,512]{1,0:T(8,128)(2,1)S(1)} %copy-done.1), custom_call_target="tpu_custom_call" | custom-call | tf_op jit(solution)/shard_map/pallas_call | solution.py:155
  34.5 1.2 %copy.5 = f32[896,512]{1,0:T(8,128)} copy(f32[896,512]{1,0:T(8,128)S(1)} %shard_map.37) | data formatting | bytes 3670016
Async XLA Ops:
  0.0 1.2 %copy-start = (f32[4,224,224]{2,1,0:T(8,128)S(1)}, f32[4,224,224]{2,1,0:T(8,128)}, u32[]{:S(2)}) copy-start(f32[4,224,224]{2,1,0:T(8,128)} %inverses.1) | copy-start | bytes 2408452
  1.2 1.2 %copy-start.1 = (bf16[896,512]{1,0:T(8,128)(2,1)S(1)}, bf16[896,512]{1,0:T(8,128)(2,1)}, u32[]{:S(2)}) copy-start(bf16[896,512]{1,0:T(8,128)(2,1)} %probes.1) | copy-start | bytes 2752516

commit v2 on v1

v2 whole, which is shorter than its diff:
```python
import functools

import jax
import jax.numpy as jnp
from jax import lax
from jax.experimental import pallas as pl
from jax.experimental.pallas import tpu as pltpu
from jax.sharding import PartitionSpec as P

MESH = pl.DeviceIdType.MESH
WIDTH = 256


def dot(a, b):
    return jnp.dot(a, b, preferred_element_type=jnp.float32)


def split(x):
    high = x.astype(jnp.bfloat16)
    return high, (x - high.astype(jnp.float32)).astype(jnp.bfloat16)


def kernel(
    panels, width, flat, lower, inverses, probes, out,
    factor, inverse, inv_high, inv_low, fold_high, fold_low, probe, result, solved, pending,
    load_sem, factor_sem, send_sem, recv_sem, out_sem,
):
    count, size = inverses.shape[0], inverses.shape[1]
    rows = count * size
    chunks = probes.shape[1] // width
    me = lax.axis_index("panel")
    after = lax.rem(me + 1, panels)
    has_next = me < panels - 1
    blocks = [slice(b * size, (b + 1) * size) for b in range(count)]

    barrier = pltpu.get_barrier_semaphore()

    @pl.when(me > 0)
    def _():
        pl.semaphore_signal(barrier, inc=1, device_id={"panel": me - 1}, device_id_type=MESH)

    def load_factor(q):
        if flat:
            source = lower.at[:, pl.ds(pl.multiple_of(q * rows, 128), rows)]
        else:
            source = lower.at[q]
        return pltpu.make_async_copy(source, factor.at[q], factor_sem.at[q])

    def block_copy(c, g):
        block = solved.at[c, pl.ds(pl.multiple_of(g * size, 16), size)]
        return pltpu.make_async_remote_copy(
            src_ref=block,
            dst_ref=block,
            send_sem=send_sem.at[c, g],
            recv_sem=recv_sem.at[c, g],
            device_id={"panel": after},
            device_id_type=MESH,
        )

    def send(c, g):
        @pl.when(has_next)
        def _():
            block_copy(c, g).start()

    def columns_of(c):
        return pl.ds(pl.multiple_of(c * width, 128), width)

    def out_copy(c, b):
        return pltpu.make_async_copy(
            result.at[blocks[b], columns_of(c)], out.at[blocks[b], columns_of(c)], out_sem.at[c, b]
        )

    def begin(c):
        for b in range(count):
            given = probe[blocks[b], columns_of(c)]
            pending[blocks[b]] = dot(inv_high[b], given) + dot(inv_low[b], given)

    def fold(q, j, first):
        for b in range(first, count):
            part = factor[q, blocks[b], blocks[j]]
            g = q * count + j
            fold_high[g, blocks[b]], fold_low[g, blocks[b]] = split(
                dot(inv_high[b], part) + dot(inv_low[b], part)
            )

    def update(c, g, first):
        block = solved[c, pl.ds(pl.multiple_of(g * size, 16), size)]
        below = slice(first * size, rows)
        pending[below] -= dot(fold_high[g, below], block) + dot(fold_low[g, below], block)

    def finalize(c, b):
        block = pending[blocks[b]]
        g = me * count + b
        solved[c, pl.ds(pl.multiple_of(g * size, 16), size)] = block.astype(jnp.bfloat16)
        send(c, g)
        result[blocks[b], columns_of(c)] = block
        out_copy(c, b).start()

    load_inverse = pltpu.make_async_copy(inverses, inverse, load_sem.at[0])
    load_probe = pltpu.make_async_copy(probes, probe, load_sem.at[1])
    load_inverse.start()
    load_probe.start()
    load_factor(me).start()

    def start_factor(q, carry):
        load_factor(q).start()
        return carry

    lax.fori_loop(0, me, start_factor, 0)
    load_inverse.wait()
    for b in range(count):
        inv_high[b], inv_low[b] = split(inverse[b])
    load_probe.wait()
    begin(0)

    @pl.when(has_next)
    def _():
        pl.semaphore_wait(barrier, 1)

    @pl.when(me == 0)
    def _():
        finalize(0, 0)

    load_factor(me).wait()
    for j in range(count - 1):
        fold(me, j, j + 1)

    def chunk(c, carry):
        @pl.when(c > 0)
        def _():
            begin(c)

        def earlier(q, carry):
            @pl.when(c == 0)
            def _():
                load_factor(q).wait()

            for j in range(count):
                g = q * count + j
                block_copy(c, g).wait_recv()
                send(c, g)

                @pl.when(c == 0)
                def _():
                    fold(q, j, 0)

                update(c, g, 0)
            return carry

        lax.fori_loop(0, me, earlier, 0)

        @pl.when(me + c > 0)
        def _():
            finalize(c, 0)

        for b in range(1, count):
            update(c, me * count + b - 1, b)
            finalize(c, b)
        return carry

    lax.fori_loop(0, chunks, chunk, 0)

    def finish(c, carry):
        for b in range(count):
            out_copy(c, b).wait()

        @pl.when(has_next)
        def _():
            def sent(g, carry):
                block_copy(c, g).wait_send()
                return carry

            lax.fori_loop(0, (me + 1) * count, sent, 0)

        return carry

    lax.fori_loop(0, chunks, finish, 0)


def per_device(lower_factor, inverses, probes):
    panels = lax.axis_size("panel")
    count, size, _ = inverses.shape
    rows, columns = probes.shape
    width = WIDTH if columns % WIDTH == 0 else columns
    chunks = columns // width
    flat = rows % 128 == 0
    if not flat:
        lower_factor = lower_factor.reshape(rows, panels, rows).transpose(1, 0, 2)
    bf16, f32 = jnp.bfloat16, jnp.float32
    dma = pltpu.SemaphoreType.DMA
    return pl.pallas_call(
        functools.partial(kernel, panels, width, flat),
        out_shape=jax.ShapeDtypeStruct((rows, columns), f32),
        in_specs=[pl.BlockSpec(memory_space=pltpu.HBM)] * 3,
        out_specs=pl.BlockSpec(memory_space=pl.ANY),
        scratch_shapes=[
            pltpu.VMEM((panels, rows, rows), bf16),
            pltpu.VMEM((count, size, size), f32),
            pltpu.VMEM((count, size, size), bf16),
            pltpu.VMEM((count, size, size), bf16),
            pltpu.VMEM((panels * count, rows, size), bf16),
            pltpu.VMEM((panels * count, rows, size), bf16),
            pltpu.VMEM((rows, columns), bf16),
            pltpu.VMEM((rows, columns), f32),
            pltpu.VMEM((chunks, panels * rows, width), bf16),
            pltpu.VMEM((rows, width), f32),
            dma((2,)),
            dma((panels,)),
            dma((chunks, panels * count)),
            dma((chunks, panels * count)),
            dma((chunks, count)),
        ],
        compiler_params=pltpu.CompilerParams(
            collective_id=0, has_side_effects=True, vmem_limit_bytes=48 * 1024 * 1024
        ),
    )(lower_factor, inverses, probes)


def solution(mesh):
    return jax.shard_map(
        per_device,
        mesh=mesh,
        in_specs=(
            P(("expert", "panel"), None),
            P(("expert", "panel"), None, None),
            P(("expert", "panel"), None),
        ),
        out_specs=P(("expert", "panel"), None),
        check_vma=False,
    )
```

time: 36 us -> 33.6 us (0.933)
  Pallas kernels: 32.2 us -> 29.8 us
    pallas_call x1, Pallas kernels: 32.2 us -> 29.8 us  [per_device(): pl.pallas_call(functools.partial(kernel, panels, width, flat), out_shape=...]
where the time goes in v2:
time: 33.6 us; the launch traced here: 33.4 us
  Pallas kernels  29.8 us (89%)
  local copies, waits for them, and re-layouts  3.59 us (11%)
    pallas_call x1, Pallas kernels, per_device(): pl.pallas_call(functools.partial(kernel, panels, width, flat), out_shape=...  29.8 us
    unnamed x5, local copies, waits for them, and re-layouts  3.59 us

profile of v2, /device:TPU:29, one launch (start us, length us, event | category | flops | bytes accessed | tf_op | source)
XLA Modules:
  0.0 33.4 jit_solution(16221293902715437901)
XLA Ops:
  0.0 0.0 copy-start
  0.0 1.2 %copy-done = f32[4,224,224]{2,1,0:T(8,128)S(1)} copy-done((f32[4,224,224]{2,1,0:T(8,128)S(1)}, f32[4,224,224]{2,1,0:T(8,128)}, u32[]{:S(2)}) %copy-start) | copy-done | bytes 802840
  1.2 0.0 copy-start.1
  1.2 1.2 %copy-done.1 = bf16[896,512]{1,0:T(8,128)(2,1)S(1)} copy-done((bf16[896,512]{1,0:T(8,128)(2,1)S(1)}, bf16[896,512]{1,0:T(8,128)(2,1)}, u32[]{:S(2)}) %copy-start.1) | copy-done | bytes 917528
  2.4 29.8 %shard_map.37 = f32[896,512]{1,0:T(8,128)S(1)} custom-call(bf16[896,3584]{1,0:T(8,128)(2,1)} %lower.1, f32[4,224,224]{2,1,0:T(8,128)S(1)} %copy-done, bf16[896,512]{1,0:T(8,128)(2,1)S(1)} %copy-done.1), custom_call_target="tpu_custom_call" | custom-call | tf_op jit(solution)/shard_map/pallas_call | solution.py:191
  32.1 1.2 %copy.5 = f32[896,512]{1,0:T(8,128)} copy(f32[896,512]{1,0:T(8,128)S(1)} %shard_map.37) | data formatting | bytes 3670016
Async XLA Ops:
  0.0 1.2 %copy-start = (f32[4,224,224]{2,1,0:T(8,128)S(1)}, f32[4,224,224]{2,1,0:T(8,128)}, u32[]{:S(2)}) copy-start(f32[4,224,224]{2,1,0:T(8,128)} %inverses.1) | copy-start | bytes 2408452
  1.2 1.2 %copy-start.1 = (bf16[896,512]{1,0:T(8,128)(2,1)S(1)}, bf16[896,512]{1,0:T(8,128)(2,1)}, u32[]{:S(2)}) copy-start(bf16[896,512]{1,0:T(8,128)(2,1)} %probes.1) | copy-start | bytes 2752516

commit v3 on v2

--- a/solution.py
+++ b/solution.py
@@ -22,7 +22,7 @@
 
 def kernel(
     panels, width, flat, lower, inverses, probes, out,
-    factor, inverse, inv_high, inv_low, fold_high, fold_low, probe, result, solved, pending,
+    factor, inverse, inv_high, inv_low, folded, probe, result, solved, pending,
     load_sem, factor_sem, send_sem, recv_sem, out_sem,
 ):
     count, size = inverses.shape[0], inverses.shape[1]
@@ -79,14 +79,12 @@
         for b in range(first, count):
             part = factor[q, blocks[b], blocks[j]]
             g = q * count + j
-            fold_high[g, blocks[b]], fold_low[g, blocks[b]] = split(
-                dot(inv_high[b], part) + dot(inv_low[b], part)
-            )
+            folded[g, blocks[b]] = (dot(inv_high[b], part) + dot(inv_low[b], part)).astype(jnp.bfloat16)
 
     def update(c, g, first):
         block = solved[c, pl.ds(pl.multiple_of(g * size, 16), size)]
         below = slice(first * size, rows)
-        pending[below] -= dot(fold_high[g, below], block) + dot(fold_low[g, below], block)
+        pending[below] -= dot(folded[g, below], block)
 
     def finalize(c, b):
         block = pending[blocks[b]]
@@ -190,7 +188,7 @@
     dma = pltpu.SemaphoreType.DMA
     return pl.pallas_call(
         functools.partial(kernel, panels, width, flat),
-        out_shape=jax.ShapeDtypeStruct((rows, columns), f32),
+        out_shape=pltpu.VMEM((rows, columns), f32),
         in_specs=[pl.BlockSpec(memory_space=pltpu.HBM)] * 3,
         out_specs=pl.BlockSpec(memory_space=pl.ANY),
         scratch_shapes=[
@@ -198,7 +196,6 @@
             pltpu.VMEM((count, size, size), f32),
             pltpu.VMEM((count, size, size), bf16),
             pltpu.VMEM((count, size, size), bf16),
-            pltpu.VMEM((panels * count, rows, size), bf16),
             pltpu.VMEM((panels * count, rows, size), bf16),
             pltpu.VMEM((rows, columns), bf16),
             pltpu.VMEM((rows, columns), f32),
@@ -211,7 +208,7 @@
             dma((chunks, count)),
         ],
         compiler_params=pltpu.CompilerParams(
-            collective_id=0, has_side_effects=True, vmem_limit_bytes=48 * 1024 * 1024
+            collective_id=0, has_side_effects=True, vmem_limit_bytes=54 * 1024 * 1024
         ),
     )(lower_factor, inverses, probes)
 

time: 33.6 us -> 30.3 us (0.902)
  local copies, waits for them, and re-layouts: 3.59 us -> 1.23 us
  Pallas kernels: 29.8 us -> 28.9 us
    unnamed x5 -> x1, local copies, waits for them, and re-layouts: 3.59 us -> 1.23 us
    pallas_call x1, Pallas kernels: 29.8 us -> 28.9 us  [per_device(): pl.pallas_call(functools.partial(kernel, panels, width, flat), out_shape=...]
where the time goes in v3:
time: 30.3 us; the launch traced here: 30.2 us
  Pallas kernels  28.9 us (95%)
  local copies, waits for them, and re-layouts  1.23 us (4%)
    pallas_call x1, Pallas kernels, per_device(): pl.pallas_call(functools.partial(kernel, panels, width, flat), out_shape=...  28.9 us
    unnamed x1, local copies, waits for them, and re-layouts  1.23 us

profile of v3, /device:TPU:29, one launch (start us, length us, event | category | flops | bytes accessed | tf_op | source)
XLA Modules:
  0.0 30.2 jit_solution(1754973447020245193)
XLA Ops:
  0.0 28.9 %shard_map.37 = f32[896,512]{1,0:T(8,128)S(1)} custom-call(bf16[896,3584]{1,0:T(8,128)(2,1)} %lower.1, f32[4,224,224]{2,1,0:T(8,128)} %inverses.1, bf16[896,512]{1,0:T(8,128)(2,1)} %probes.1), custom_call_target="tpu_custom_call" | custom-call | tf_op jit(solution)/shard_map/pallas_call | solution.py:189
  28.9 1.2 %copy.5 = f32[896,512]{1,0:T(8,128)} copy(f32[896,512]{1,0:T(8,128)S(1)} %shard_map.37) | data formatting | bytes 3670016

commit v4 on v3

--- a/solution.py
+++ b/solution.py
@@ -22,8 +22,8 @@
 
 def kernel(
     panels, width, flat, lower, inverses, probes, out,
-    factor, inverse, inv_high, inv_low, folded, probe, result, solved, pending,
-    load_sem, factor_sem, send_sem, recv_sem, out_sem,
+    factor, inverse, inv_high, inv_low, fold_high, fold_low, probe, solved, pending,
+    load_sem, factor_sem, send_sem, recv_sem,
 ):
     count, size = inverses.shape[0], inverses.shape[1]
     rows = count * size
@@ -65,34 +65,37 @@
     def columns_of(c):
         return pl.ds(pl.multiple_of(c * width, 128), width)
 
-    def out_copy(c, b):
-        return pltpu.make_async_copy(
-            result.at[blocks[b], columns_of(c)], out.at[blocks[b], columns_of(c)], out_sem.at[c, b]
-        )
-
     def begin(c):
         for b in range(count):
             given = probe[blocks[b], columns_of(c)]
             pending[blocks[b]] = dot(inv_high[b], given) + dot(inv_low[b], given)
 
+    def in_two(j, first):
+        return first == 0 and (j < count - 1 or count == 1)
+
     def fold(q, j, first):
         for b in range(first, count):
             part = factor[q, blocks[b], blocks[j]]
             g = q * count + j
-            folded[g, blocks[b]] = (dot(inv_high[b], part) + dot(inv_low[b], part)).astype(jnp.bfloat16)
-
-    def update(c, g, first):
+            high, low = split(dot(inv_high[b], part) + dot(inv_low[b], part))
+            fold_high[g, blocks[b]] = high
+            if in_two(j, first):
+                fold_low[g, blocks[b]] = low
+
+    def update(c, g, first, two=False):
         block = solved[c, pl.ds(pl.multiple_of(g * size, 16), size)]
         below = slice(first * size, rows)
-        pending[below] -= dot(folded[g, below], block)
+        change = dot(fold_high[g, below], block)
+        if two:
+            change += dot(fold_low[g, below], block)
+        pending[below] -= change
 
     def finalize(c, b):
         block = pending[blocks[b]]
         g = me * count + b
         solved[c, pl.ds(pl.multiple_of(g * size, 16), size)] = block.astype(jnp.bfloat16)
         send(c, g)
-        result[blocks[b], columns_of(c)] = block
-        out_copy(c, b).start()
+        out[blocks[b], columns_of(c)] = block
 
     load_inverse = pltpu.make_async_copy(inverses, inverse, load_sem.at[0])
     load_probe = pltpu.make_async_copy(probes, probe, load_sem.at[1])
@@ -142,7 +145,7 @@
                 def _():
                     fold(q, j, 0)
 
-                update(c, g, 0)
+                update(c, g, 0, in_two(j, 0))
             return carry
 
         lax.fori_loop(0, me, earlier, 0)
@@ -159,9 +162,6 @@
     lax.fori_loop(0, chunks, chunk, 0)
 
     def finish(c, carry):
-        for b in range(count):
-            out_copy(c, b).wait()
-
         @pl.when(has_next)
         def _():
             def sent(g, carry):
@@ -190,22 +190,21 @@
         functools.partial(kernel, panels, width, flat),
         out_shape=pltpu.VMEM((rows, columns), f32),
         in_specs=[pl.BlockSpec(memory_space=pltpu.HBM)] * 3,
-        out_specs=pl.BlockSpec(memory_space=pl.ANY),
+        out_specs=pl.BlockSpec(memory_space=pltpu.VMEM),
         scratch_shapes=[
             pltpu.VMEM((panels, rows, rows), bf16),
             pltpu.VMEM((count, size, size), f32),
             pltpu.VMEM((count, size, size), bf16),
             pltpu.VMEM((count, size, size), bf16),
             pltpu.VMEM((panels * count, rows, size), bf16),
+            pltpu.VMEM((panels * count, rows, size), bf16),
             pltpu.VMEM((rows, columns), bf16),
-            pltpu.VMEM((rows, columns), f32),
             pltpu.VMEM((chunks, panels * rows, width), bf16),
             pltpu.VMEM((rows, width), f32),
             dma((2,)),
             dma((panels,)),
             dma((chunks, panels * count)),
             dma((chunks, panels * count)),
-            dma((chunks, count)),
         ],
         compiler_params=pltpu.CompilerParams(
             collective_id=0, has_side_effects=True, vmem_limit_bytes=54 * 1024 * 1024

time: 30.3 us -> 30.3 us (level)
  no operation moved by 1% of the time
where the time goes in v4:
time: 30.3 us; the launch traced here: 30.2 us
  Pallas kernels  28.9 us (95%)
  local copies, waits for them, and re-layouts  1.23 us (4%)
    pallas_call x1, Pallas kernels, per_device(): pl.pallas_call(functools.partial(kernel, panels, width, flat), out_shape=...  28.9 us
    unnamed x1, local copies, waits for them, and re-layouts  1.23 us

profile of v4, /device:TPU:29, one launch (start us, length us, event | category | flops | bytes accessed | tf_op | source)
XLA Modules:
  0.0 30.2 jit_solution(9529673234959829067)
XLA Ops:
  0.0 28.9 %shard_map.37 = f32[896,512]{1,0:T(8,128)S(1)} custom-call(bf16[896,3584]{1,0:T(8,128)(2,1)} %lower.1, f32[4,224,224]{2,1,0:T(8,128)} %inverses.1, bf16[896,512]{1,0:T(8,128)(2,1)} %probes.1), custom_call_target="tpu_custom_call" | custom-call | tf_op jit(solution)/shard_map/pallas_call | solution.py:189
  29.0 1.2 %copy.5 = f32[896,512]{1,0:T(8,128)} copy(f32[896,512]{1,0:T(8,128)S(1)} %shard_map.37) | data formatting | bytes 3670016

commit v5 on v3

--- a/solution.py
+++ b/solution.py
@@ -22,8 +22,8 @@
 
 def kernel(
     panels, width, flat, lower, inverses, probes, out,
-    factor, inverse, inv_high, inv_low, folded, probe, result, solved, pending,
-    load_sem, factor_sem, send_sem, recv_sem, out_sem,
+    factor, inverse, inv_high, inv_low, folded, probe, solved, pending,
+    load_sem, factor_sem, send_sem, recv_sem,
 ):
     count, size = inverses.shape[0], inverses.shape[1]
     rows = count * size
@@ -65,11 +65,6 @@
     def columns_of(c):
         return pl.ds(pl.multiple_of(c * width, 128), width)
 
-    def out_copy(c, b):
-        return pltpu.make_async_copy(
-            result.at[blocks[b], columns_of(c)], out.at[blocks[b], columns_of(c)], out_sem.at[c, b]
-        )
-
     def begin(c):
         for b in range(count):
             given = probe[blocks[b], columns_of(c)]
@@ -91,8 +86,7 @@
         g = me * count + b
         solved[c, pl.ds(pl.multiple_of(g * size, 16), size)] = block.astype(jnp.bfloat16)
         send(c, g)
-        result[blocks[b], columns_of(c)] = block
-        out_copy(c, b).start()
+        out[blocks[b], columns_of(c)] = block
 
     load_inverse = pltpu.make_async_copy(inverses, inverse, load_sem.at[0])
     load_probe = pltpu.make_async_copy(probes, probe, load_sem.at[1])
@@ -159,9 +153,6 @@
     lax.fori_loop(0, chunks, chunk, 0)
 
     def finish(c, carry):
-        for b in range(count):
-            out_copy(c, b).wait()
-
         @pl.when(has_next)
         def _():
             def sent(g, carry):
@@ -190,7 +181,7 @@
         functools.partial(kernel, panels, width, flat),
         out_shape=pltpu.VMEM((rows, columns), f32),
         in_specs=[pl.BlockSpec(memory_space=pltpu.HBM)] * 3,
-        out_specs=pl.BlockSpec(memory_space=pl.ANY),
+        out_specs=pl.BlockSpec(memory_space=pltpu.VMEM),
         scratch_shapes=[
             pltpu.VMEM((panels, rows, rows), bf16),
             pltpu.VMEM((count, size, size), f32),
@@ -198,14 +189,12 @@
             pltpu.VMEM((count, size, size), bf16),
             pltpu.VMEM((panels * count, rows, size), bf16),
             pltpu.VMEM((rows, columns), bf16),
-            pltpu.VMEM((rows, columns), f32),
             pltpu.VMEM((chunks, panels * rows, width), bf16),
             pltpu.VMEM((rows, width), f32),
             dma((2,)),
             dma((panels,)),
             dma((chunks, panels * count)),
             dma((chunks, panels * count)),
-            dma((chunks, count)),
         ],
         compiler_params=pltpu.CompilerParams(
             collective_id=0, has_side_effects=True, vmem_limit_bytes=54 * 1024 * 1024

time: 30.3 us -> 30 us (0.990)
  no operation moved by 1% of the time
where the time goes in v5:
time: 30 us; the launch traced here: 29.9 us
  Pallas kernels  28.7 us (96%)
  local copies, waits for them, and re-layouts  1.23 us (4%)
    pallas_call x1, Pallas kernels, per_device(): pl.pallas_call(functools.partial(kernel, panels, width, flat), out_shape=...  28.7 us
    unnamed x1, local copies, waits for them, and re-layouts  1.23 us

profile of v5, /device:TPU:29, one launch (start us, length us, event | category | flops | bytes accessed | tf_op | source)
XLA Modules:
  0.0 29.9 jit_solution(13707478584164439691)
XLA Ops:
  0.0 28.7 %shard_map.37 = f32[896,512]{1,0:T(8,128)S(1)} custom-call(bf16[896,3584]{1,0:T(8,128)(2,1)} %lower.1, f32[4,224,224]{2,1,0:T(8,128)} %inverses.1, bf16[896,512]{1,0:T(8,128)(2,1)} %probes.1), custom_call_target="tpu_custom_call" | custom-call | tf_op jit(solution)/shard_map/pallas_call | solution.py:180
  28.7 1.2 %copy.5 = f32[896,512]{1,0:T(8,128)} copy(f32[896,512]{1,0:T(8,128)S(1)} %shard_map.37) | data formatting | bytes 3670016
